TPU v7x, 32 devices: a whole 2x2x4 slice. The times are simulated.
32 devices in a mesh: parts: 2 (over y), chain: 4 (over x, core), group: 4 (over z).
Axes of the slice: x: 2, y: 2, z: 4, core: 2. Of those that a mesh axis runs over, the one named last changes fastest.
Arguments:
- rhs: float32 [8, 5, 64, 64], P(('parts', 'chain'), None, None, 'group'), parts along dimension 0, may hold values from -6 to 6
- inv_block: float32 [8, 64, 320, 320], P(('parts', 'chain'), 'group'), parts along dimension 0, may hold values from -0.3125 to 0.3125
- flux_jac: float32 [8, 3, 5, 5, 64], P(('parts', 'chain'), None, None, None, 'group'), parts along dimension 0, may hold values from -2.5 to 2.5
- up_elem: int32 [8, 3, 64], P(('parts', 'chain'), None, 'group'), parts along dimension 0, may hold values from 0 to 63, each once within a row
- lift: float32 [3, 64, 16], replicated, may hold values from -0.875 to 0.875
Outputs:
- solution: float32 [8, 5, 64, 64], P(('parts', 'chain'), None, None, 'group'), parts along dimension 0
There are 2 independent parts, one for each index of `parts`. A program takes and returns all parts, laid end to end along the dimension named above; an argument that names none is the same for every part. Nothing has to cross between parts.
Inputs may be any that keep to these rules, and one draw needn't show every extreme that they name: For every section s and face k, up_elem[s, k, :] names each of the 64 elements once; row s = 0 is not read.
All inputs are finite; a program needn't handle non-finite values.
Results may differ from a plain program's by a relative error of at most 0.02.
Values may be sent and summed in bfloat16 or wider, within the bound.
A program may use at most 64 MiB of HBM per device.

v0:
```python
import jax
import jax.numpy as jnp
from jax import lax
from jax.sharding import PartitionSpec as P

VARS = 5
NP = 4
NODES = 64
FACE = 16


HIGH = lax.Precision.HIGHEST


def passed_along(value, axis, steps):
    count = lax.axis_size(axis)
    initial, last = (max(0, -steps), min(count, count - steps))
    return lax.ppermute(value, axis, [(source, source + steps) for source in range(initial, last)])


def face_traces(solved):
    elements = solved.shape[-1]
    cube = solved.reshape(VARS, NP, NP, NP, elements)
    first = cube[:, NP - 1, :, :, :].reshape(VARS, FACE, elements)
    second = cube[:, :, NP - 1, :, :].reshape(VARS, FACE, elements)
    third = cube[:, :, :, NP - 1, :].reshape(VARS, FACE, elements)
    return jnp.stack([first, second, third]).astype(jnp.bfloat16)


def solve_section(rhs_s, inv_s, jac_s, up_s, prev_full, lift):
    elements = rhs_s.shape[-1]
    picked = jnp.stack([jnp.take(prev_full[k], up_s[k], axis=2) for k in range(3)])
    upstream = picked.astype(jnp.float32)
    mixed = jnp.einsum("kwve,kvfe->kwfe", jac_s, upstream, precision=HIGH)
    coupling = jnp.einsum("kif,kwfe->wie", lift, mixed, precision=HIGH)
    flat = (rhs_s - coupling).reshape(VARS * NODES, elements)
    result = jnp.einsum("eij,je->ie", inv_s, flat, precision=HIGH)
    return result.reshape(VARS, NODES, elements)


def body(rhs, inv_block, flux_jac, up_elem, lift):
    local = rhs.shape[3]
    chains = lax.axis_size("chain")

    def chain_step(turn, carry):
        last_traces, solved_all = carry
        previous = passed_along(last_traces, "chain", 1)
        full_front = lax.all_gather(previous, "group", axis=3, tiled=True)
        solved = solve_section(rhs[0], inv_block[0], flux_jac[0], up_elem[0], full_front, lift)
        solved_list = [solved]
        previous = face_traces(solved)
        return (previous, jnp.stack(solved_list))

    start = (jnp.zeros((3, VARS, FACE, local), jnp.bfloat16), jnp.zeros(rhs.shape, jnp.float32))
    ended, solution = lax.fori_loop(0, chains, chain_step, start)
    return solution


def solution(mesh):
    return jax.shard_map(
        body,
        mesh=mesh,
        in_specs=(
            P(("parts", "chain"), None, None, "group"),
            P(("parts", "chain"), "group", None, None),
            P(("parts", "chain"), None, None, None, "group"),
            P(("parts", "chain"), None, "group"),
            P(),
        ),
        out_specs=P(("parts", "chain"), None, None, "group"),
        check_vma=False,
    )
```

profile of v0, /device:TPU:6, one launch (start us, length us, event | category | flops | bytes accessed | tf_op | source)
XLA Modules:
  0.0 141.1 jit_solution(16525215014715003966)
XLA Ops:
  0.0 0.8 copy.30
  0.8 0.7 copy.29
  1.5 138.1 %while.12 = (s32[]{:T(128)}, bf16[3,5,16,16]{3,2,1,0:T(8,128)(2,1)S(1)}, f32[1,5,64,16]{2,1,3,0:T(8,128)}, f32[1,5,64,16]{2,3,1,0:T(8,128)}, s32[1,3,16]{2,1,0:T...) while((s32[]{:T(128)}, ...), condition=%wide.region_1.3_spmd, body=%wide.region_0.2_spmd.sunk | while | flops 22868000 | bytes 7120933 | solution.py:55
  1.6 1.9 %collective-permute-start = (bf16[3,5,16,16]{2,1,3,0:T(8,128)(2,1)S(1)}, bf16[3,5,16,16]{2,1,3,0:T(8,128)(2,1)S(1)}, u32[]{:S(2)}, u32[]{:S(2)}) collective-permute-start(bf16[3,5,16,16]{2,1,3,0:T(8,128)(2,1)S(1)} %copy.50), channel_id=1, source_target_pairs={{0,4},{4,8},{8,12},{1,5},{5,9},{9,13},{2,6},{6,10},{10,14},{3,7},{... | collective-permute-start | bytes 23048 | tf_op jit(solution)/shard_map/while/body/eval_jaxpr/ppermute | solution.py:18
  3.8 3.8 %collective-permute-done = bf16[3,5,16,16]{2,1,3,0:T(8,128)(2,1)S(1)} collective-permute-done((bf16[3,5,16,16]{2,1,3,0:T(8,128)(2,1)S(1)}, bf16[3,5,16,16]{2,1,3,0:T(8,128)(2,1)S(1)}, u32[]{:S(2)}, u32[]{:S(2)}) %collective-permute-start) | collective-permute-done | bytes 7712 | tf_op jit(solution)/shard_map/while/body/eval_jaxpr/ppermute | solution.py:18
  7.6 15.4 %all_gather.4 = bf16[3,5,16,64]{2,1,3,0:T(8,128)(2,1)S(1)} all-gather(bf16[3,5,16,16]{2,1,3,0:T(8,128)(2,1)S(1)} %collective-permute-done), channel_id=1, replica_groups=mesh['parts'=2,'chain'=4,'group'=4] {'group'}, dimensions={3}, use_global_device_ids=true | all-gather | bytes 38400 | tf_op jit(solution)/shard_map/while/body/eval_jaxpr/all_gather | solution.py:48
  23.0 0.6 gather_fusion.1
  25.3 1.1 fusion.27
  26.5 9.1 %fusion.28 = f32[16,1,320]{2,1,0:T(1,128)S(1)} fusion(f32[320,16,1]{0,2,1:T(1,128)S(1)} %reshape.74, f32[1,16,320,320]{3,2,1,0:T(8,128)} %get-tuple-element.205), kind=kOutput, calls=%fused_computation.3.clone.1 | convolution fusion | flops 19660800 | bytes 6594560 | tf_op jit(solution)/shard_map/while/body/eval_jaxpr/eij,je->ie/dot_general | solution.py:37
  35.8 0.7 reshape.75
  36.7 1.9 %collective-permute-start = (bf16[3,5,16,16]{2,1,3,0:T(8,128)(2,1)S(1)}, bf16[3,5,16,16]{2,1,3,0:T(8,128)(2,1)S(1)}, u32[]{:S(2)}, u32[]{:S(2)}) collective-permute-start(bf16[3,5,16,16]{2,1,3,0:T(8,128)(2,1)S(1)} %copy.50), channel_id=1, source_target_pairs={{0,4},{4,8},{8,12},{1,5},{5,9},{9,13},{2,6},{6,10},{10,14},{3,7},{... | collective-permute-start | bytes 23048 | tf_op jit(solution)/shard_map/while/body/eval_jaxpr/ppermute | solution.py:18
  38.9 3.8 %collective-permute-done = bf16[3,5,16,16]{2,1,3,0:T(8,128)(2,1)S(1)} collective-permute-done((bf16[3,5,16,16]{2,1,3,0:T(8,128)(2,1)S(1)}, bf16[3,5,16,16]{2,1,3,0:T(8,128)(2,1)S(1)}, u32[]{:S(2)}, u32[]{:S(2)}) %collective-permute-start) | collective-permute-done | bytes 7712 | tf_op jit(solution)/shard_map/while/body/eval_jaxpr/ppermute | solution.py:18
  42.6 15.1 %all_gather.4 = bf16[3,5,16,64]{2,1,3,0:T(8,128)(2,1)S(1)} all-gather(bf16[3,5,16,16]{2,1,3,0:T(8,128)(2,1)S(1)} %collective-permute-done), channel_id=1, replica_groups=mesh['parts'=2,'chain'=4,'group'=4] {'group'}, dimensions={3}, use_global_device_ids=true | all-gather | bytes 38400 | tf_op jit(solution)/shard_map/while/body/eval_jaxpr/all_gather | solution.py:48
  57.9 0.6 gather_fusion.1
  60.1 1.1 fusion.27
  61.3 9.1 %fusion.28 = f32[16,1,320]{2,1,0:T(1,128)S(1)} fusion(f32[320,16,1]{0,2,1:T(1,128)S(1)} %reshape.74, f32[1,16,320,320]{3,2,1,0:T(8,128)} %get-tuple-element.205), kind=kOutput, calls=%fused_computation.3.clone.1 | convolution fusion | flops 19660800 | bytes 6594560 | tf_op jit(solution)/shard_map/while/body/eval_jaxpr/eij,je->ie/dot_general | solution.py:37
  70.7 0.7 reshape.75
  71.5 1.9 %collective-permute-start = (bf16[3,5,16,16]{2,1,3,0:T(8,128)(2,1)S(1)}, bf16[3,5,16,16]{2,1,3,0:T(8,128)(2,1)S(1)}, u32[]{:S(2)}, u32[]{:S(2)}) collective-permute-start(bf16[3,5,16,16]{2,1,3,0:T(8,128)(2,1)S(1)} %copy.50), channel_id=1, source_target_pairs={{0,4},{4,8},{8,12},{1,5},{5,9},{9,13},{2,6},{6,10},{10,14},{3,7},{... | collective-permute-start | bytes 23048 | tf_op jit(solution)/shard_map/while/body/eval_jaxpr/ppermute | solution.py:18
  73.7 3.8 %collective-permute-done = bf16[3,5,16,16]{2,1,3,0:T(8,128)(2,1)S(1)} collective-permute-done((bf16[3,5,16,16]{2,1,3,0:T(8,128)(2,1)S(1)}, bf16[3,5,16,16]{2,1,3,0:T(8,128)(2,1)S(1)}, u32[]{:S(2)}, u32[]{:S(2)}) %collective-permute-start) | collective-permute-done | bytes 7712 | tf_op jit(solution)/shard_map/while/body/eval_jaxpr/ppermute | solution.py:18
  77.5 14.5 %all_gather.4 = bf16[3,5,16,64]{2,1,3,0:T(8,128)(2,1)S(1)} all-gather(bf16[3,5,16,16]{2,1,3,0:T(8,128)(2,1)S(1)} %collective-permute-done), channel_id=1, replica_groups=mesh['parts'=2,'chain'=4,'group'=4] {'group'}, dimensions={3}, use_global_device_ids=true | all-gather | bytes 38400 | tf_op jit(solution)/shard_map/while/body/eval_jaxpr/all_gather | solution.py:48
  92.0 0.6 gather_fusion.1
  94.3 1.1 fusion.27
  95.5 9.1 %fusion.28 = f32[16,1,320]{2,1,0:T(1,128)S(1)} fusion(f32[320,16,1]{0,2,1:T(1,128)S(1)} %reshape.74, f32[1,16,320,320]{3,2,1,0:T(8,128)} %get-tuple-element.205), kind=kOutput, calls=%fused_computation.3.clone.1 | convolution fusion | flops 19660800 | bytes 6594560 | tf_op jit(solution)/shard_map/while/body/eval_jaxpr/eij,je->ie/dot_general | solution.py:37
  104.9 0.7 reshape.75
  105.7 1.9 %collective-permute-start = (bf16[3,5,16,16]{2,1,3,0:T(8,128)(2,1)S(1)}, bf16[3,5,16,16]{2,1,3,0:T(8,128)(2,1)S(1)}, u32[]{:S(2)}, u32[]{:S(2)}) collective-permute-start(bf16[3,5,16,16]{2,1,3,0:T(8,128)(2,1)S(1)} %copy.50), channel_id=1, source_target_pairs={{0,4},{4,8},{8,12},{1,5},{5,9},{9,13},{2,6},{6,10},{10,14},{3,7},{... | collective-permute-start | bytes 23048 | tf_op jit(solution)/shard_map/while/body/eval_jaxpr/ppermute | solution.py:18
  107.9 3.8 %collective-permute-done = bf16[3,5,16,16]{2,1,3,0:T(8,128)(2,1)S(1)} collective-permute-done((bf16[3,5,16,16]{2,1,3,0:T(8,128)(2,1)S(1)}, bf16[3,5,16,16]{2,1,3,0:T(8,128)(2,1)S(1)}, u32[]{:S(2)}, u32[]{:S(2)}) %collective-permute-start) | collective-permute-done | bytes 7712 | tf_op jit(solution)/shard_map/while/body/eval_jaxpr/ppermute | solution.py:18
  111.7 14.4 %all_gather.4 = bf16[3,5,16,64]{2,1,3,0:T(8,128)(2,1)S(1)} all-gather(bf16[3,5,16,16]{2,1,3,0:T(8,128)(2,1)S(1)} %collective-permute-done), channel_id=1, replica_groups=mesh['parts'=2,'chain'=4,'group'=4] {'group'}, dimensions={3}, use_global_device_ids=true | all-gather | bytes 38400 | tf_op jit(solution)/shard_map/while/body/eval_jaxpr/all_gather | solution.py:48
  126.1 0.6 gather_fusion.1
  128.3 1.1 fusion.27
  129.5 9.1 %fusion.28 = f32[16,1,320]{2,1,0:T(1,128)S(1)} fusion(f32[320,16,1]{0,2,1:T(1,128)S(1)} %reshape.74, f32[1,16,320,320]{3,2,1,0:T(8,128)} %get-tuple-element.205), kind=kOutput, calls=%fused_computation.3.clone.1 | convolution fusion | flops 19660800 | bytes 6594560 | tf_op jit(solution)/shard_map/while/body/eval_jaxpr/eij,je->ie/dot_general | solution.py:37
  138.9 0.7 reshape.75
  139.6 1.5 %copy.31 = f32[1,5,64,16]{2,3,1,0:T(8,128)} copy(f32[1,5,64,16]{2,1,3,0:T(8,128)} %get-tuple-element.47) | data formatting | bytes 40960 | tf_op jit(solution)/shard_map/while | solution.py:55
  (86 shorter events, 9.6 us)
Async XLA Ops:
  1.6 5.9 %collective-permute-start = (bf16[3,5,16,16]{2,1,3,0:T(8,128)(2,1)S(1)}, bf16[3,5,16,16]{2,1,3,0:T(8,128)(2,1)S(1)}, u32[]{:S(2)}, u32[]{:S(2)}) collective-permute-start(bf16[3,5,16,16]{2,1,3,0:T(8,128)(2,1)S(1)} %copy.50), channel_id=1, source_target_pairs={{0,4},{4,8},{8,12},{1,5},{5,9},{9,13},{2,6},{6,10},{10,14},{3,7},{... | collective-permute-start | bytes 23048 | tf_op jit(solution)/shard_map/while/body/eval_jaxpr/ppermute | solution.py:18
  36.7 5.9 %collective-permute-start = (bf16[3,5,16,16]{2,1,3,0:T(8,128)(2,1)S(1)}, bf16[3,5,16,16]{2,1,3,0:T(8,128)(2,1)S(1)}, u32[]{:S(2)}, u32[]{:S(2)}) collective-permute-start(bf16[3,5,16,16]{2,1,3,0:T(8,128)(2,1)S(1)} %copy.50), channel_id=1, source_target_pairs={{0,4},{4,8},{8,12},{1,5},{5,9},{9,13},{2,6},{6,10},{10,14},{3,7},{... | collective-permute-start | bytes 23048 | tf_op jit(solution)/shard_map/while/body/eval_jaxpr/ppermute | solution.py:18
  71.5 5.9 %collective-permute-start = (bf16[3,5,16,16]{2,1,3,0:T(8,128)(2,1)S(1)}, bf16[3,5,16,16]{2,1,3,0:T(8,128)(2,1)S(1)}, u32[]{:S(2)}, u32[]{:S(2)}) collective-permute-start(bf16[3,5,16,16]{2,1,3,0:T(8,128)(2,1)S(1)} %copy.50), channel_id=1, source_target_pairs={{0,4},{4,8},{8,12},{1,5},{5,9},{9,13},{2,6},{6,10},{10,14},{3,7},{... | collective-permute-start | bytes 23048 | tf_op jit(solution)/shard_map/while/body/eval_jaxpr/ppermute | solution.py:18
  105.7 5.9 %collective-permute-start = (bf16[3,5,16,16]{2,1,3,0:T(8,128)(2,1)S(1)}, bf16[3,5,16,16]{2,1,3,0:T(8,128)(2,1)S(1)}, u32[]{:S(2)}, u32[]{:S(2)}) collective-permute-start(bf16[3,5,16,16]{2,1,3,0:T(8,128)(2,1)S(1)} %copy.50), channel_id=1, source_target_pairs={{0,4},{4,8},{8,12},{1,5},{5,9},{9,13},{2,6},{6,10},{10,14},{3,7},{... | collective-permute-start | bytes 23048 | tf_op jit(solution)/shard_map/while/body/eval_jaxpr/ppermute | solution.py:18
where the time goes:
time: 142 us; the launch traced here: 141 us
  blocking collectives  59.4 us (42%)
  matrix products  42 us (30%)
  local copies, waits for them, and re-layouts  15.4 us (11%)
  waiting for transfers between devices  15.1 us (11%)
  starting transfers between devices  7.68 us (5%)
    all_gather x4, blocking collectives, chain_step(): full_front = lax.all_gather(previous, 'group', axis=3, tiled=True)  59.4 us
    dot_general x4, matrix products, solve_section(): result = jnp.einsum('eij,je->ie', inv_s, flat, precision=HIGH)  36.5 us
    ppermute x4, waiting for transfers between devices, passed_along(): lax.ppermute(value, axis, [(source, source + steps) for source in range(i...  15.1 us
    ppermute x4, starting transfers between devices, passed_along(): lax.ppermute(value, axis, [(source, source + steps) for source in range(i...  7.68 us
    gather x12, local copies, waits for them, and re-layouts, solve_section(): jnp.take(prev_full[k], up_s[k], axis=2)  6.88 us
    dot_general x4, matrix products, solve_section(): coupling = jnp.einsum('kif,kwfe->wie', lift, mixed, precision=HIGH)  4.27 us
    while x3, local copies, waits for them, and re-layouts, body(): ended, solution = lax.fori_loop(0, chains, chain_step, start)  2.94 us
  transfers between devices with their start and end apart: 4, of which 4 were waited for; matrix products, arithmetic and copies ran while one was open for 1% of the time, Pallas kernels for 0%

commit v1 on v0

v1 whole, which is shorter than its diff:
```python
import functools

import jax
import jax.numpy as jnp
from jax import lax
from jax.experimental import pallas as pl
from jax.experimental.pallas import tpu as pltpu
from jax.sharding import PartitionSpec as P

VARS = 5
NODES = 64
FACE = 16
BLOCK = VARS * NODES
FACES = 3
LANES = 128
WIDE = FACES * LANES
SHIFTS = tuple(range(1 - VARS, VARS))
MESH = pl.DeviceIdType.MESH
F32 = jnp.float32
BF16 = jnp.bfloat16


def iota(shape, axis):
    return lax.broadcasted_iota(jnp.int32, shape, axis)


def select_operator(k):
    col = iota((BLOCK, LANES), 1)
    f = col & 15
    if k == 0:
        node = 48 + f
    elif k == 1:
        node = ((f >> 2) << 4) + 12 + (f & 3)
    else:
        node = (f << 2) + 3
    wanted = ((col >> 4) << 6) + node
    return jnp.where(iota((BLOCK, LANES), 0) == wanted, 1.0, 0.0).astype(BF16)


def kernel(chains, groups, local, rhs_hbm, inv_hbm, jac_hbm, up_hbm, lift_hbm, out_hbm,
           rhs_v, inv_v, jac_v, up_v, lift_v, out_v, invb, sel, liftb, mix, hot, res, outgoing, incoming,
           small_sem, inv_sem, out_sem, send_sem, recv_sem):
    s = lax.axis_index("chain")
    g = lax.axis_index("group")
    small = [
        pltpu.make_async_copy(src, dst, small_sem.at[n])
        for n, (src, dst) in enumerate(
            ((up_hbm.at[0], up_v), (jac_hbm.at[0], jac_v), (lift_hbm, lift_v), (rhs_hbm.at[0], rhs_v))
        )
    ]
    for copy in small:
        copy.start()
    blocks = [pltpu.make_async_copy(inv_hbm.at[0, e], inv_v.at[e], inv_sem.at[e]) for e in range(local)]
    for copy in blocks:
        copy.start()

    barrier = pltpu.get_barrier_semaphore()

    @pl.when(s > 0)
    def _():
        for other in range(groups):
            pl.semaphore_signal(
                barrier, inc=1, device_id={"chain": s - 1, "group": other}, device_id_type=MESH
            )

    for k in range(FACES):
        sel[:, k * LANES:(k + 1) * LANES] = select_operator(k)

    for copy in small:
        copy.wait()

    res[...] = jnp.transpose(rhs_v[...].reshape(BLOCK, local))

    @pl.when(s > 0)
    def _():
        elements = groups * local
        slot = iota((local, LANES), 1) >> 4
        for k in range(FACES):
            match = jnp.where(iota((elements, local), 0) == up_v[k:k + 1, :], 1.0, 0.0)
            hot[k] = jnp.transpose(match).astype(BF16)
            part = jnp.transpose(lift_v[k])
            wide = jnp.concatenate([part] * VARS, axis=1)
            place = iota((FACE, BLOCK), 1) >> 6
            for w in range(VARS):
                liftb[k * LANES + w * FACE:k * LANES + (w + 1) * FACE, :] = jnp.where(
                    place == w, wide, 0.0
                ).astype(BF16)
            liftb[k * LANES + VARS * FACE:(k + 1) * LANES, :] = jnp.zeros(
                (LANES - VARS * FACE, BLOCK), BF16
            )
            columns = [jnp.transpose(jac_v[k, w]) for w in range(VARS)]
            for n, d in enumerate(SHIFTS):
                total = jnp.zeros((local, LANES), F32)
                for w in range(VARS):
                    if 0 <= w - d < VARS:
                        total = jnp.where(slot == w, columns[w][:, w - d:w - d + 1], total)
                mix[k, n] = total

    for e in range(local):
        blocks[e].wait()
        invb[e] = inv_v[e].astype(BF16)

    @pl.when(s > 0)
    def _():
        for other in range(groups):
            pltpu.make_async_remote_copy(
                src_ref=outgoing,
                dst_ref=incoming.at[pl.ds(other * local, local), :],
                send_sem=send_sem.at[other],
                recv_sem=recv_sem.at[other],
                device_id={"chain": s - 1, "group": other},
                device_id_type=MESH,
            ).wait_recv()
        mixed = []
        for k in range(FACES):
            u = jnp.dot(hot[k], incoming[:, k * LANES:(k + 1) * LANES], preferred_element_type=F32)
            total = jnp.zeros((local, LANES), F32)
            for n, d in enumerate(SHIFTS):
                moved = u if d == 0 else pltpu.roll(u, (d * FACE) % LANES, 1)
                total = total + moved * mix[k, n]
            mixed.append(total.astype(BF16))
        coupling = jnp.dot(jnp.concatenate(mixed, axis=1), liftb[...], preferred_element_type=F32)
        res[...] = res[...] - coupling

    given = res[...].astype(BF16)
    row = iota((local, BLOCK), 0)
    solved = jnp.zeros((local, BLOCK), F32)
    for e in range(local):
        one = lax.dot_general(given, invb[e], (((1,), (1,)), ((), ())), preferred_element_type=F32)
        solved = jnp.where(row == e, one, solved)
    traces = jnp.dot(solved.astype(BF16), sel[...], preferred_element_type=F32)
    outgoing[...] = traces.astype(BF16)

    def sends():
        return [
            pltpu.make_async_remote_copy(
                src_ref=outgoing,
                dst_ref=incoming.at[pl.ds(pl.multiple_of(g * local, local), local), :],
                send_sem=send_sem.at[other],
                recv_sem=recv_sem.at[g],
                device_id={"chain": s + 1, "group": other},
                device_id_type=MESH,
            )
            for other in range(groups)
        ]

    @pl.when(s < chains - 1)
    def _():
        pl.semaphore_wait(barrier, groups)
        for copy in sends():
            copy.start()

    out_v[...] = jnp.transpose(solved).reshape(VARS, NODES, local)
    result = pltpu.make_async_copy(out_v, out_hbm.at[0], out_sem)
    result.start()

    @pl.when(s < chains - 1)
    def _():
        for copy in sends():
            copy.wait_send()

    result.wait()


def body(chains, groups, rhs, inv_block, flux_jac, up_elem, lift):
    local = rhs.shape[3]
    elements = groups * local
    anywhere = pl.BlockSpec(memory_space=pl.ANY)
    return pl.pallas_call(
        functools.partial(kernel, chains, groups, local),
        out_shape=jax.ShapeDtypeStruct(rhs.shape, F32),
        in_specs=[anywhere] * 5,
        out_specs=anywhere,
        scratch_shapes=[
            pltpu.VMEM((VARS, NODES, local), F32),
            pltpu.VMEM((local, BLOCK, BLOCK), F32),
            pltpu.VMEM((FACES, VARS, VARS, local), F32),
            pltpu.VMEM((FACES, local), jnp.int32),
            pltpu.VMEM((FACES, NODES, FACE), F32),
            pltpu.VMEM((VARS, NODES, local), F32),
            pltpu.VMEM((local, BLOCK, BLOCK), BF16),
            pltpu.VMEM((BLOCK, WIDE), BF16),
            pltpu.VMEM((WIDE, BLOCK), BF16),
            pltpu.VMEM((FACES, len(SHIFTS), local, LANES), F32),
            pltpu.VMEM((FACES, local, elements), BF16),
            pltpu.VMEM((local, BLOCK), F32),
            pltpu.VMEM((local, WIDE), BF16),
            pltpu.VMEM((elements, WIDE), BF16),
            pltpu.SemaphoreType.DMA((4,)),
            pltpu.SemaphoreType.DMA((local,)),
            pltpu.SemaphoreType.DMA,
            pltpu.SemaphoreType.DMA((groups,)),
            pltpu.SemaphoreType.DMA((groups,)),
        ],
        compiler_params=pltpu.CompilerParams(
            collective_id=0, has_side_effects=True, vmem_limit_bytes=40 * 1024 * 1024
        ),
    )(rhs, inv_block, flux_jac, up_elem, lift)


def solution(mesh):
    return jax.shard_map(
        functools.partial(body, mesh.shape["chain"], mesh.shape["group"]),
        mesh=mesh,
        in_specs=(
            P(("parts", "chain"), None, None, "group"),
            P(("parts", "chain"), "group", None, None),
            P(("parts", "chain"), None, None, None, "group"),
            P(("parts", "chain"), None, "group"),
            P(),
        ),
        out_specs=P(("parts", "chain"), None, None, "group"),
        check_vma=False,
    )
```

time: 142 us -> 32.3 us (0.23)
  the two profiles are of different devices: /device:TPU:6 before, /device:TPU:7 now
where the time goes in v1:
time: 32.3 us; the launch traced here: 32 us
  Pallas kernels  24.8 us (77%)
  local copies, waits for them, and re-layouts  7.12 us (22%)
    pallas_call x1, Pallas kernels, body(): pl.pallas_call(functools.partial(kernel, chains, groups, local), out_shap...  24.8 us
    unnamed x6, local copies, waits for them, and re-layouts  6.4 us
    pallas_call x1, local copies, waits for them, and re-layouts, body(): pl.pallas_call(functools.partial(kernel, chains, groups, local), out_shap...  0.72 us

profile of v1, /device:TPU:7, one launch (start us, length us, event | category | flops | bytes accessed | tf_op | source)
XLA Modules:
  0.0 32.0 jit_solution(9146028055069632742)
XLA Ops:
  0.0 0.7 %copy.8.up_hbm = s32[1,3,16]{2,1,0:T(4,128)S(1)} copy(s32[1,3,16]{2,0,1:T(1,128)} %param.8) | data formatting | bytes 384 | tf_op args[3]
  0.7 0.8 %copy.7.jac_hbm = f32[1,3,5,5,16]{4,3,2,1,0:T(8,128)S(1)} copy(f32[1,3,5,5,16]{4,0,3,2,1:T(1,128)} %param.7) | data formatting | bytes 9600 | tf_op args[2]
  1.5 0.8 %copy.9.lift_hbm = f32[3,64,16]{2,1,0:T(8,128)S(1)} copy(f32[3,64,16]{1,2,0:T(8,128)} %param.9) | data formatting | bytes 24576 | tf_op args[4]
  2.3 0.9 %copy.6.rhs_hbm = f32[1,5,64,16]{3,2,1,0:T(8,128)S(1)} copy(f32[1,5,64,16]{2,3,1,0:T(8,128)} %param.5) | data formatting | bytes 40960 | tf_op args[0]
  3.2 0.0 copy-start
  3.2 3.2 %copy-done = f32[1,16,320,320]{3,2,1,0:T(8,128)S(1)} copy-done((f32[1,16,320,320]{3,2,1,0:T(8,128)S(1)}, f32[1,16,320,320]{3,2,1,0:T(8,128)}, u32[]{:S(2)}) %copy-start) | copy-done | bytes 6553624
  6.4 24.8 %shard_map.55 = f32[1,5,64,16]{3,2,1,0:T(8,128)S(1)} custom-call(f32[1,5,64,16]{3,2,1,0:T(8,128)S(1)} %copy.6.rhs_hbm, f32[1,16,320,320]{3,2,1,0:T(8,128)S(1)} %copy-done, f32[1,3,5,5,16]{4,3,2,1,0:T(8,128)S(1)} %copy.7.jac_hbm, s32[1,3,16]{2,1,0:T(4,128)S(1)} %copy.8.up_hbm, f32[3,64,16]{2,1,0:T(8,128)S(1)} %copy.9.lift_hbm), custom_call_target="tpu_custom_call" | custom-call | tf_op jit(solution)/shard_map/pallas_call | solution.py:169
  31.2 0.7 %copy.10 = f32[1,5,64,16]{2,3,1,0:T(8,128)} copy(f32[1,5,64,16]{3,2,1,0:T(8,128)S(1)} %shard_map.55) | data formatting | bytes 40960 | tf_op jit(solution)/shard_map/pallas_call | solution.py:169
Async XLA Ops:
  3.2 3.2 %copy-start = (f32[1,16,320,320]{3,2,1,0:T(8,128)S(1)}, f32[1,16,320,320]{3,2,1,0:T(8,128)}, u32[]{:S(2)}) copy-start(f32[1,16,320,320]{3,2,1,0:T(8,128)} %inv_hbm.1) | copy-start | bytes 19660804

commit v2 on v1

v2 whole, which is shorter than its diff:
```python
import functools

import jax
import jax.numpy as jnp
from jax import lax
from jax.experimental import pallas as pl
from jax.experimental.pallas import tpu as pltpu
from jax.sharding import PartitionSpec as P

VARS = 5
NODES = 64
FACE = 16
BLOCK = VARS * NODES
FACES = 3
SIDE = VARS * FACE
USED = FACES * SIDE
WIDE = 256
MESH = pl.DeviceIdType.MESH
F32 = jnp.float32
BF16 = jnp.bfloat16


def iota(shape, axis):
    return lax.broadcasted_iota(jnp.int32, shape, axis)


def select_operator():
    shape = (BLOCK, WIDE)
    col = iota(shape, 1)
    second, third = col >= SIDE, col >= 2 * SIDE
    rest = col - jnp.where(third, 2 * SIDE, jnp.where(second, SIDE, 0))
    f = rest & 15
    node = jnp.where(third, (f << 2) + 3, jnp.where(second, ((f >> 2) << 4) + 12 + (f & 3), 48 + f))
    wanted = jnp.where(col < USED, ((rest >> 4) << 6) + node, BLOCK)
    return jnp.where(iota(shape, 0) == wanted, 1.0, 0.0).astype(BF16)


def halves(x):
    high = x.astype(BF16)
    return high, (x - high.astype(F32)).astype(BF16)


def times_transposed(a, b):
    return lax.dot_general(a, b, (((1,), (1,)), ((), ())), preferred_element_type=F32)


def face_rows(block):
    rows = []
    cube = block[...]
    rows.append(cube.reshape(VARS, NODES, BLOCK)[:, NODES - FACE:, :].reshape(SIDE, BLOCK))
    rows.append(cube.reshape(VARS * 4, 16, BLOCK)[:, 12:, :].reshape(SIDE, BLOCK))
    rows.append(cube.reshape(SIDE, 4, BLOCK)[:, 3, :])
    return jnp.concatenate(rows, axis=0)


def kernel(chains, groups, local, rhs_hbm, inv_hbm, jac_hbm, up_hbm, lift_hbm, out_hbm,
           rhs_v, inv_v, jac_v, up_v, lift_v, out_v, sel, wide_lift, coeff, hot, given, base, base_t, full, short,
           outgoing, incoming, small_sem, inv_sem, out_sem, send_sem, recv_sem):
    s = lax.axis_index("chain")
    g = lax.axis_index("group")
    last = chains - 1
    small = [
        pltpu.make_async_copy(src, dst, small_sem.at[n])
        for n, (src, dst) in enumerate(
            ((up_hbm, up_v), (jac_hbm, jac_v), (lift_hbm, lift_v), (rhs_hbm.at[0], rhs_v))
        )
    ]
    for copy in small:
        copy.start()
    blocks = [pltpu.make_async_copy(inv_hbm.at[0, e], inv_v.at[e], inv_sem.at[e]) for e in range(local)]
    for copy in blocks:
        copy.start()

    barrier = pltpu.get_barrier_semaphore()

    @pl.when(s > 0)
    def _():
        for other in range(groups):
            pl.semaphore_signal(
                barrier, inc=1, device_id={"chain": s - 1, "group": other}, device_id_type=MESH
            )

    row = iota((local, BLOCK), 0)
    row_t = iota((local, WIDE), 0)
    sel[...] = select_operator()
    for copy in small:
        copy.wait()
    high, low = halves(jnp.concatenate([rhs_v[v] for v in range(VARS)], axis=1))
    given[:local, :] = high
    given[local:, :] = low

    @pl.when(s > 0)
    def _():
        elements = groups * local
        for k in range(FACES):
            match = jnp.where(iota((elements, local), 0) == up_v[k], 1.0, 0.0)
            hot[k * local:(k + 1) * local, :] = jnp.transpose(match).astype(BF16)
            wide_lift[k] = jnp.concatenate([lift_v[k]] * VARS, axis=1)
        jac = jnp.transpose(jac_v[...].reshape(FACES * VARS * VARS, local))
        place = iota((local, BLOCK), 1) >> 6
        for k in range(FACES):
            for v in range(VARS):
                total = jnp.zeros((local, BLOCK), F32)
                for w in range(VARS):
                    at = (k * VARS + w) * VARS + v
                    total = jnp.where(place == w, jac[:, at:at + 1], total)
                coeff[k * VARS + v] = total

    def operator(e):
        return jnp.concatenate(
            [
                (wide_lift[n // VARS] * coeff[n, e:e + 1, :]).astype(BF16)
                for n in range(FACES * VARS)
            ],
            axis=0,
        )

    def pick(rows, product, e, before):
        return jnp.where(rows == e, product, before)

    def own_parts(block):
        product = times_transposed(given[...], block)
        return product[:local] + product[local:]

    def full_operators():
        solved = jnp.zeros((local, BLOCK), F32)
        for e in range(local):
            block = inv_v[e].astype(BF16)
            product = times_transposed(jnp.concatenate([operator(e), given[...]], axis=0), block)
            full[e] = product[:USED].astype(BF16)
            solved = pick(row, product[USED:USED + local] + product[USED + local:], e, solved)
        base[...] = solved

    def send_copies():
        return [
            pltpu.make_async_remote_copy(
                src_ref=outgoing,
                dst_ref=incoming.at[pl.ds(pl.multiple_of(g * local, local), local), :],
                send_sem=send_sem.at[other],
                recv_sem=recv_sem.at[g],
                device_id={"chain": s + 1, "group": other},
                device_id_type=MESH,
            )
            for other in range(groups)
        ]

    def store(solved):
        for v in range(VARS):
            out_v[v] = solved[:, v * NODES:(v + 1) * NODES]

    def send(traces):
        outgoing[...] = traces.astype(BF16)
        pl.semaphore_wait(barrier, groups)
        for copy in send_copies():
            copy.start()

    def gathered():
        for other in range(groups):
            pltpu.make_async_remote_copy(
                src_ref=outgoing,
                dst_ref=incoming.at[pl.ds(other * local, local), :],
                send_sem=send_sem.at[other],
                recv_sem=recv_sem.at[other],
                device_id={"chain": s - 1, "group": other},
                device_id_type=MESH,
            ).wait_recv()
        found = jnp.dot(hot[...], incoming[...], preferred_element_type=F32)
        lane = iota((local, WIDE), 1)
        mixed = jnp.where(
            lane < SIDE, found[:local], jnp.where(lane < 2 * SIDE, found[local:2 * local], found[2 * local:])
        )
        return mixed.astype(BF16)[:, :USED]

    def whole(u):
        coupling = jnp.zeros((local, BLOCK), F32)
        for e in range(local):
            coupling = pick(row, jnp.dot(u, full[e], preferred_element_type=F32), e, coupling)
        store(base[...] - coupling)

    @pl.when(s == 0)
    def _():
        solved = jnp.zeros((local, BLOCK), F32)
        for e in range(local):
            blocks[e].wait()
            solved = pick(row, own_parts(inv_v[e].astype(BF16)), e, solved)
        if chains > 1:
            send(jnp.dot(solved.astype(BF16), sel[...], preferred_element_type=F32))
        store(solved)

    @pl.when((s > 0) & (s < last))
    def _():
        solved = jnp.zeros((local, WIDE), F32)
        for e in range(local):
            blocks[e].wait()
            block = jnp.concatenate(
                [face_rows(inv_v.at[e]).astype(BF16), jnp.zeros((WIDE - USED, BLOCK), BF16)], axis=0
            )
            product = times_transposed(jnp.concatenate([operator(e), given[...]], axis=0), block)
            short[e] = product[:USED].astype(BF16)
            solved = pick(row_t, product[USED:USED + local] + product[USED + local:], e, solved)
        base_t[...] = solved

    @pl.when(s == last)
    def _():
        if chains > 1:
            for e in range(local):
                blocks[e].wait()

    @pl.when(s > 1)
    def _():
        full_operators()

    @pl.when((s > 0) & (s < last))
    def _():
        u = gathered()
        coupling = jnp.zeros((local, WIDE), F32)
        for e in range(local):
            coupling = pick(row_t, jnp.dot(u, short[e], preferred_element_type=F32), e, coupling)
        send(base_t[...] - coupling)

        @pl.when(s == 1)
        def _():
            full_operators()

        whole(u)

    @pl.when((s == last) & (s > 0))
    def _():
        if chains == 2:
            full_operators()
        whole(gathered())

    result = pltpu.make_async_copy(out_v, out_hbm.at[0], out_sem)
    result.start()

    @pl.when(s < last)
    def _():
        for copy in send_copies():
            copy.wait_send()

    result.wait()


def body(chains, groups, rhs, inv_block, flux_jac, up_elem, lift):
    local = rhs.shape[3]
    elements = groups * local
    anywhere = pl.BlockSpec(memory_space=pl.ANY)
    solved = pl.pallas_call(
        functools.partial(kernel, chains, groups, local),
        out_shape=jax.ShapeDtypeStruct((1, VARS, local, NODES), F32),
        in_specs=[anywhere] * 5,
        out_specs=anywhere,
        scratch_shapes=[
            pltpu.VMEM((VARS, local, NODES), F32),
            pltpu.VMEM((local, BLOCK, BLOCK), F32),
            pltpu.VMEM((FACES * VARS * VARS, 1, local), F32),
            pltpu.VMEM((FACES, 1, local), jnp.int32),
            pltpu.VMEM((FACES, FACE, NODES), F32),
            pltpu.VMEM((VARS, local, NODES), F32),
            pltpu.VMEM((BLOCK, WIDE), BF16),
            pltpu.VMEM((FACES, FACE, BLOCK), F32),
            pltpu.VMEM((FACES * VARS, local, BLOCK), F32),
            pltpu.VMEM((FACES * local, elements), BF16),
            pltpu.VMEM((2 * local, BLOCK), BF16),
            pltpu.VMEM((local, BLOCK), F32),
            pltpu.VMEM((local, WIDE), F32),
            pltpu.VMEM((local, USED, BLOCK), BF16),
            pltpu.VMEM((local, USED, WIDE), BF16),
            pltpu.VMEM((local, WIDE), BF16),
            pltpu.VMEM((elements, WIDE), BF16),
            pltpu.SemaphoreType.DMA((4,)),
            pltpu.SemaphoreType.DMA((local,)),
            pltpu.SemaphoreType.DMA,
            pltpu.SemaphoreType.DMA((groups,)),
            pltpu.SemaphoreType.DMA((groups,)),
        ],
        compiler_params=pltpu.CompilerParams(
            collective_id=0, has_side_effects=True, vmem_limit_bytes=58 * 1024 * 1024
        ),
    )(
        jnp.transpose(rhs, (0, 1, 3, 2)),
        inv_block,
        jnp.transpose(flux_jac, (1, 2, 3, 0, 4)).reshape(FACES * VARS * VARS, 1, local),
        jnp.transpose(up_elem, (1, 0, 2)),
        jnp.transpose(lift, (0, 2, 1)),
    )
    return jnp.transpose(solved, (0, 1, 3, 2))


def solution(mesh):
    return jax.shard_map(
        functools.partial(body, mesh.shape["chain"], mesh.shape["group"]),
        mesh=mesh,
        in_specs=(
            P(("parts", "chain"), None, None, "group"),
            P(("parts", "chain"), "group", None, None),
            P(("parts", "chain"), None, None, None, "group"),
            P(("parts", "chain"), None, "group"),
            P(),
        ),
        out_specs=P(("parts", "chain"), None, None, "group"),
        check_vma=False,
    )
```

time: 32.3 us -> 22.6 us (0.70)
  local copies, waits for them, and re-layouts: 7.12 us -> 1.4 us
  Pallas kernels: 24.8 us -> 21 us
    unnamed x6 -> x1, local copies, waits for them, and re-layouts: 6.4 us -> 1.4 us
    pallas_call x1, Pallas kernels: 24.8 us -> 21 us  [body(): pl.pallas_call(functools.partial(kernel, chains, groups, local), out_shap...]
    pallas_call x1 -> x0, local copies, waits for them, and re-layouts: 0.72 us -> none  [body(): pl.pallas_call(functools.partial(kernel, chains, groups, local), out_shap...]
where the time goes in v2:
time: 22.6 us; the launch traced here: 22.4 us
  Pallas kernels  21 us (93%)
  local copies, waits for them, and re-layouts  1.4 us (6%)
    pallas_call x1, Pallas kernels, body(): pl.pallas_call(functools.partial(kernel, chains, groups, local), out_shap...  21 us
    unnamed x1, local copies, waits for them, and re-layouts  1.4 us

profile of v2, /device:TPU:7, one launch (start us, length us, event | category | flops | bytes accessed | tf_op | source)
XLA Modules:
  0.0 22.4 jit_solution(8633499524544119834)
XLA Ops:
  0.0 21.0 %shard_map.55 = f32[1,5,16,64]{3,2,1,0:T(8,128)} custom-call(f32[1,5,16,64]{3,2,1,0:T(8,128)} %bitcast.6, f32[1,16,320,320]{3,2,1,0:T(8,128)} %inv_hbm.1, f32[75,1,16]{2,1,0:T(1,128)} %bitcast.7, s32[3,1,16]{2,1,0:T(1,128)} %bitcast.9, f32[3,16,64]{2,1,0:T(8,128)} %bitcast.8), custom_call_target="tpu_custom_call" | custom-call | tf_op jit(solution)/shard_map/pallas_call | solution.py:248
  21.0 1.4 %copy.7 = f32[1,5,64,16]{2,3,1,0:T(8,128)} copy(f32[1,5,64,16]{2,3,1,0:T(8,128)} %bitcast.5) | data formatting | bytes 40960

commit v3 on v2

--- a/solution.py
+++ b/solution.py
@@ -54,7 +54,7 @@
 
 
 def kernel(chains, groups, local, rhs_hbm, inv_hbm, jac_hbm, up_hbm, lift_hbm, out_hbm,
-           rhs_v, inv_v, jac_v, up_v, lift_v, out_v, sel, wide_lift, coeff, hot, given, base, base_t, full, short,
+           rhs_v, inv_v, jac_v, up_v, lift_v, out_v, sel, wide_lift, coeff, hot, given, base, base_t, kept, short,
            outgoing, incoming, small_sem, inv_sem, out_sem, send_sem, recv_sem):
     s = lax.axis_index("chain")
     g = lax.axis_index("group")
@@ -118,16 +118,28 @@
     def pick(rows, product, e, before):
         return jnp.where(rows == e, product, before)
 
-    def own_parts(block):
-        product = times_transposed(given[...], block)
-        return product[:local] + product[local:]
+    def solve(right, arriving):
+        high, low = halves(right)
+        columns = jnp.transpose(
+            jnp.concatenate([high.astype(F32), low.astype(F32)], axis=0)
+        ).astype(BF16)
+        lane = iota((BLOCK, 2 * local), 1)
+        total = jnp.zeros((BLOCK, 2 * local), F32)
+        for e in range(local):
+            if arriving is not None:
+                arriving[e].wait()
+            block = inv_v[e].astype(BF16)
+            product = jnp.dot(block, columns, preferred_element_type=F32)
+            total = jnp.where((lane == e) | (lane == e + local), product, total)
+        return jnp.transpose(total[:, :local] + total[:, local:])
 
     def full_operators():
         solved = jnp.zeros((local, BLOCK), F32)
         for e in range(local):
+            blocks[e].wait()
             block = inv_v[e].astype(BF16)
             product = times_transposed(jnp.concatenate([operator(e), given[...]], axis=0), block)
-            full[e] = product[:USED].astype(BF16)
+            kept[e] = product[:USED].astype(BF16)
             solved = pick(row, product[USED:USED + local] + product[USED + local:], e, solved)
         base[...] = solved
 
@@ -171,18 +183,18 @@
         )
         return mixed.astype(BF16)[:, :USED]
 
-    def whole(u):
+    def coupled(u):
         coupling = jnp.zeros((local, BLOCK), F32)
         for e in range(local):
-            coupling = pick(row, jnp.dot(u, full[e], preferred_element_type=F32), e, coupling)
-        store(base[...] - coupling)
+            coupling = pick(row, jnp.dot(u, kept[e], preferred_element_type=F32), e, coupling)
+        return coupling
+
+    def right_sides():
+        return jnp.concatenate([rhs_v[v] for v in range(VARS)], axis=1)
 
     @pl.when(s == 0)
     def _():
-        solved = jnp.zeros((local, BLOCK), F32)
-        for e in range(local):
-            blocks[e].wait()
-            solved = pick(row, own_parts(inv_v[e].astype(BF16)), e, solved)
+        solved = solve(right_sides(), blocks)
         if chains > 1:
             send(jnp.dot(solved.astype(BF16), sel[...], preferred_element_type=F32))
         store(solved)
@@ -195,40 +207,23 @@
             block = jnp.concatenate(
                 [face_rows(inv_v.at[e]).astype(BF16), jnp.zeros((WIDE - USED, BLOCK), BF16)], axis=0
             )
-            product = times_transposed(jnp.concatenate([operator(e), given[...]], axis=0), block)
+            own = operator(e)
+            kept[e] = own
+            product = times_transposed(jnp.concatenate([own, given[...]], axis=0), block)
             short[e] = product[:USED].astype(BF16)
             solved = pick(row_t, product[USED:USED + local] + product[USED + local:], e, solved)
         base_t[...] = solved
-
-    @pl.when(s == last)
-    def _():
-        if chains > 1:
-            for e in range(local):
-                blocks[e].wait()
-
-    @pl.when(s > 1)
-    def _():
-        full_operators()
-
-    @pl.when((s > 0) & (s < last))
-    def _():
         u = gathered()
         coupling = jnp.zeros((local, WIDE), F32)
         for e in range(local):
             coupling = pick(row_t, jnp.dot(u, short[e], preferred_element_type=F32), e, coupling)
         send(base_t[...] - coupling)
-
-        @pl.when(s == 1)
-        def _():
-            full_operators()
-
-        whole(u)
+        store(solve(right_sides() - coupled(u), None))
 
     @pl.when((s == last) & (s > 0))
     def _():
-        if chains == 2:
-            full_operators()
-        whole(gathered())
+        full_operators()
+        store(base[...] - coupled(gathered()))
 
     result = pltpu.make_async_copy(out_v, out_hbm.at[0], out_sem)
     result.start()

time: 22.6 us -> 23 us (1.018)
  Pallas kernels: 21 us -> 21.5 us
    pallas_call x1, Pallas kernels: 21 us -> 21.5 us  [body(): pl.pallas_call(functools.partial(kernel, chains, groups, local), out_shap...]
where the time goes in v3:
time: 23 us; the launch traced here: 22.9 us
  Pallas kernels  21.5 us (93%)
  local copies, waits for them, and re-layouts  1.4 us (6%)
    pallas_call x1, Pallas kernels, body(): pl.pallas_call(functools.partial(kernel, chains, groups, local), out_shap...  21.5 us
    unnamed x1, local copies, waits for them, and re-layouts  1.4 us

profile of v3, /device:TPU:7, one launch (start us, length us, event | category | flops | bytes accessed | tf_op | source)
XLA Modules:
  0.0 22.9 jit_solution(17178324267536432362)
XLA Ops:
  0.0 21.5 %shard_map.55 = f32[1,5,16,64]{3,2,1,0:T(8,128)} custom-call(f32[1,5,16,64]{3,2,1,0:T(8,128)} %bitcast.6, f32[1,16,320,320]{3,2,1,0:T(8,128)} %inv_hbm.1, f32[75,1,16]{2,1,0:T(1,128)} %bitcast.7, s32[3,1,16]{2,1,0:T(1,128)} %bitcast.9, f32[3,16,64]{2,1,0:T(8,128)} %bitcast.8), custom_call_target="tpu_custom_call" | custom-call | tf_op jit(solution)/shard_map/pallas_call | solution.py:243
  21.5 1.4 %copy.7 = f32[1,5,64,16]{2,3,1,0:T(8,128)} copy(f32[1,5,64,16]{2,3,1,0:T(8,128)} %bitcast.5) | data formatting | bytes 40960

commit v4 on v3

--- a/solution.py
+++ b/solution.py
@@ -15,6 +15,7 @@
 SIDE = VARS * FACE
 USED = FACES * SIDE
 WIDE = 256
+BATCH = 4
 MESH = pl.DeviceIdType.MESH
 F32 = jnp.float32
 BF16 = jnp.bfloat16
@@ -115,10 +116,15 @@
             axis=0,
         )
 
+    def arrive(e):
+        if e % BATCH == 0:
+            for block in blocks[e:e + BATCH]:
+                block.wait()
+
     def pick(rows, product, e, before):
         return jnp.where(rows == e, product, before)
 
-    def solve(right, arriving):
+    def solve(right):
         high, low = halves(right)
         columns = jnp.transpose(
             jnp.concatenate([high.astype(F32), low.astype(F32)], axis=0)
@@ -126,8 +132,6 @@
         lane = iota((BLOCK, 2 * local), 1)
         total = jnp.zeros((BLOCK, 2 * local), F32)
         for e in range(local):
-            if arriving is not None:
-                arriving[e].wait()
             block = inv_v[e].astype(BF16)
             product = jnp.dot(block, columns, preferred_element_type=F32)
             total = jnp.where((lane == e) | (lane == e + local), product, total)
@@ -136,7 +140,7 @@
     def full_operators():
         solved = jnp.zeros((local, BLOCK), F32)
         for e in range(local):
-            blocks[e].wait()
+            arrive(e)
             block = inv_v[e].astype(BF16)
             product = times_transposed(jnp.concatenate([operator(e), given[...]], axis=0), block)
             kept[e] = product[:USED].astype(BF16)
@@ -194,7 +198,11 @@
 
     @pl.when(s == 0)
     def _():
-        solved = solve(right_sides(), blocks)
+        solved = jnp.zeros((local, BLOCK), F32)
+        for e in range(local):
+            arrive(e)
+            product = times_transposed(given[...], inv_v[e].astype(BF16))
+            solved = pick(row, product[:local] + product[local:], e, solved)
         if chains > 1:
             send(jnp.dot(solved.astype(BF16), sel[...], preferred_element_type=F32))
         store(solved)
@@ -203,7 +211,7 @@
     def _():
         solved = jnp.zeros((local, WIDE), F32)
         for e in range(local):
-            blocks[e].wait()
+            arrive(e)
             block = jnp.concatenate(
                 [face_rows(inv_v.at[e]).astype(BF16), jnp.zeros((WIDE - USED, BLOCK), BF16)], axis=0
             )
@@ -218,7 +226,7 @@
         for e in range(local):
             coupling = pick(row_t, jnp.dot(u, short[e], preferred_element_type=F32), e, coupling)
         send(base_t[...] - coupling)
-        store(solve(right_sides() - coupled(u), None))
+        store(solve(right_sides() - coupled(u)))
 
     @pl.when((s == last) & (s > 0))
     def _():

time: 23 us -> 20.6 us (0.90)
  Pallas kernels: 21.5 us -> 19.1 us
    pallas_call x1, Pallas kernels: 21.5 us -> 19.1 us  [body(): pl.pallas_call(functools.partial(kernel, chains, groups, local), out_shap...]
where the time goes in v4:
time: 20.6 us; the launch traced here: 20.5 us
  Pallas kernels  19.1 us (93%)
  local copies, waits for them, and re-layouts  1.4 us (7%)
    pallas_call x1, Pallas kernels, body(): pl.pallas_call(functools.partial(kernel, chains, groups, local), out_shap...  19.1 us
    unnamed x1, local copies, waits for them, and re-layouts  1.4 us

profile of v4, /device:TPU:7, one launch (start us, length us, event | category | flops | bytes accessed | tf_op | source)
XLA Modules:
  0.0 20.5 jit_solution(6601391143374528363)
XLA Ops:
  0.0 19.1 %shard_map.55 = f32[1,5,16,64]{3,2,1,0:T(8,128)} custom-call(f32[1,5,16,64]{3,2,1,0:T(8,128)} %bitcast.6, f32[1,16,320,320]{3,2,1,0:T(8,128)} %inv_hbm.1, f32[75,1,16]{2,1,0:T(1,128)} %bitcast.7, s32[3,1,16]{2,1,0:T(1,128)} %bitcast.9, f32[3,16,64]{2,1,0:T(8,128)} %bitcast.8), custom_call_target="tpu_custom_call" | custom-call | tf_op jit(solution)/shard_map/pallas_call | solution.py:251
  19.1 1.4 %copy.7 = f32[1,5,64,16]{2,3,1,0:T(8,128)} copy(f32[1,5,64,16]{2,3,1,0:T(8,128)} %bitcast.5) | data formatting | bytes 40960

commit v5 on v4

--- a/solution.py
+++ b/solution.py
@@ -15,7 +15,8 @@
 SIDE = VARS * FACE
 USED = FACES * SIDE
 WIDE = 256
-BATCH = 4
+FIRST_BATCH = 4
+BATCH = 8
 MESH = pl.DeviceIdType.MESH
 F32 = jnp.float32
 BF16 = jnp.bfloat16
@@ -116,9 +117,9 @@
             axis=0,
         )
 
-    def arrive(e):
-        if e % BATCH == 0:
-            for block in blocks[e:e + BATCH]:
+    def arrive(e, batch):
+        if e % batch == 0:
+            for block in blocks[e:e + batch]:
                 block.wait()
 
     def pick(rows, product, e, before):
@@ -140,7 +141,7 @@
     def full_operators():
         solved = jnp.zeros((local, BLOCK), F32)
         for e in range(local):
-            arrive(e)
+            arrive(e, BATCH)
             block = inv_v[e].astype(BF16)
             product = times_transposed(jnp.concatenate([operator(e), given[...]], axis=0), block)
             kept[e] = product[:USED].astype(BF16)
@@ -200,7 +201,7 @@
     def _():
         solved = jnp.zeros((local, BLOCK), F32)
         for e in range(local):
-            arrive(e)
+            arrive(e, FIRST_BATCH)
             product = times_transposed(given[...], inv_v[e].astype(BF16))
             solved = pick(row, product[:local] + product[local:], e, solved)
         if chains > 1:
@@ -211,7 +212,7 @@
     def _():
         solved = jnp.zeros((local, WIDE), F32)
         for e in range(local):
-            arrive(e)
+            arrive(e, BATCH)
             block = jnp.concatenate(
                 [face_rows(inv_v.at[e]).astype(BF16), jnp.zeros((WIDE - USED, BLOCK), BF16)], axis=0
             )

time: 20.6 us -> 20.6 us (level)
  no operation moved by 1% of the time
where the time goes in v5:
time: 20.6 us; the launch traced here: 20.5 us
  Pallas kernels  19.1 us (93%)
  local copies, waits for them, and re-layouts  1.4 us (7%)
    pallas_call x1, Pallas kernels, body(): pl.pallas_call(functools.partial(kernel, chains, groups, local), out_shap...  19.1 us
    unnamed x1, local copies, waits for them, and re-layouts  1.4 us

profile of v5, /device:TPU:7, one launch (start us, length us, event | category | flops | bytes accessed | tf_op | source)
XLA Modules:
  0.0 20.5 jit_solution(6979861675033192879)
XLA Ops:
  0.0 19.1 %shard_map.55 = f32[1,5,16,64]{3,2,1,0:T(8,128)} custom-call(f32[1,5,16,64]{3,2,1,0:T(8,128)} %bitcast.6, f32[1,16,320,320]{3,2,1,0:T(8,128)} %inv_hbm.1, f32[75,1,16]{2,1,0:T(1,128)} %bitcast.7, s32[3,1,16]{2,1,0:T(1,128)} %bitcast.9, f32[3,16,64]{2,1,0:T(8,128)} %bitcast.8), custom_call_target="tpu_custom_call" | custom-call | tf_op jit(solution)/shard_map/pallas_call | solution.py:252
  19.1 1.4 %copy.7 = f32[1,5,64,16]{2,3,1,0:T(8,128)} copy(f32[1,5,64,16]{2,3,1,0:T(8,128)} %bitcast.5) | data formatting | bytes 40960
